TPU v7x, 128 devices: a whole 4x4x4 slice. The times are simulated.
128 devices in a mesh: req: 4 (over x), tile: 32 (over z, y, core).
Axes of the slice: x: 4, y: 4, z: 4, core: 2. Of those that a mesh axis runs over, the one named last changes fastest.
Arguments:
- latents: bfloat16 [8, 128, 80, 512], P('req', 'tile'), may hold values from -6 to 6
- lengths: int32 [4], replicated, may hold values from 1 to 4, 8 in all
- conv_first: bfloat16 [3, 3, 3, 512, 512], replicated, may hold values from -0.0546875 to 0.0546875
- conv_second: bfloat16 [3, 3, 3, 512, 512], replicated, may hold values from -0.0546875 to 0.0546875
- gain_first: float32 [512], replicated, may hold values from 0.1 to 1.9
- gain_second: float32 [512], replicated, may hold values from 0.1 to 1.9
Outputs:
- block_out: bfloat16 [8, 128, 80, 512], P('req', 'tile')
Inputs may be any that keep to these rules, and one draw needn't show every extreme that they name: The lengths sum to 8; the longest clip has exactly 4 frames.
All inputs are finite; a program needn't handle non-finite values.
Results may differ from a plain program's by a relative error of at most 0.0038.
Values may be sent and summed in bfloat16 or wider, within the bound.
A program may use at most 128 MiB of HBM per device.

v0:
```python
import jax
import jax.numpy as jnp
from jax import lax
from jax.sharding import PartitionSpec as P

GROUPS = 32


def passed_along(block, axis, distance):
    devices = range(lax.axis_size(axis))
    route = [(i - distance, i) for i in devices if i - distance in devices]
    return lax.ppermute(block, axis, route)


def with_halo(block, sides, width):
    for axis, dim in sides:
        count = lax.axis_size(axis)
        forward = [(i, i + 1) for i in range(count - 1)]
        backward = [(target, source) for source, target in forward]
        low = lax.ppermute(
            lax.slice_in_dim(block, block.shape[dim] - width, None, axis=dim), axis, forward
        )
        high = lax.ppermute(lax.slice_in_dim(block, 0, width, axis=dim), axis, backward)
        block = jnp.concatenate([low, block, high], axis=dim)
    return block


def clip_ids(slot_ids, lengths):
    starts = jnp.cumsum(lengths) - lengths
    return jnp.sum((slot_ids[:, None] >= starts[None, :]).astype(jnp.int32), axis=1) - 1


def group_stats(field, member, lengths, height, width):
    chans = field.shape[3]
    per_group = chans // GROUPS
    total = jnp.sum(field.astype(jnp.float32), axis=(1, 2))
    squares = jnp.sum(jnp.square(field.astype(jnp.float32)), axis=(1, 2))
    clip_total = jnp.dot(member.T, total, precision=lax.Precision.HIGHEST)
    clip_squares = jnp.dot(member.T, squares, precision=lax.Precision.HIGHEST)
    summed_total, summed_squares = lax.psum((clip_total, clip_squares), ("req", "tile"))
    group_total = jnp.sum(summed_total.reshape(-1, GROUPS, per_group), axis=2)
    group_squares = jnp.sum(summed_squares.reshape(-1, GROUPS, per_group), axis=2)
    counts = lengths.astype(jnp.float32) * (height * width * per_group)
    mean = group_total / counts[:, None]
    rstd = lax.rsqrt(group_squares / counts[:, None] - mean * mean + 1e-06)
    mean_frame = jnp.dot(
        member, jnp.repeat(mean, per_group, axis=1), precision=lax.Precision.HIGHEST
    )
    rstd_frame = jnp.dot(
        member, jnp.repeat(rstd, per_group, axis=1), precision=lax.Precision.HIGHEST
    )
    return (mean_frame, rstd_frame)


def activate(field, mean_frame, rstd_frame, gain, valid_rows):
    scaled = (
        (field.astype(jnp.float32) - mean_frame[:, None, None, :])
        * rstd_frame[:, None, None, :]
        * gain
    )
    return (jax.nn.silu(scaled) * valid_rows).astype(jnp.bfloat16)


def extend_frames(act):
    earlier = passed_along(act, "req", 1)
    return jnp.concatenate([earlier, act], axis=0)


def row_faces(extended):
    return with_halo(extended, (("tile", 1),), 1)


def causal_conv(extended, kernel, causal):
    frames = extended.shape[0] - 2
    rows = extended.shape[1] - 2
    width = extended.shape[2]
    chans = extended.shape[3]
    padded = jnp.pad(extended, ((0, 0), (0, 0), (1, 1), (0, 0)))
    pieces = [padded[:, dy : dy + rows, dx : dx + width, :] for dy in range(3) for dx in range(3)]
    columns = jnp.concatenate(pieces, axis=-1)
    taps = kernel.reshape(3, 9 * chans, chans)
    total = jnp.zeros((frames, rows, width, chans), jnp.float32)
    for dt in range(3):
        block = columns[dt : dt + frames].reshape(frames * rows * width, 9 * chans)
        product = jnp.dot(block, taps[dt], preferred_element_type=jnp.float32).reshape(
            frames, rows, width, chans
        )
        total = total + causal[dt][:, None, None, None] * product
    return total


def shards(latents, lengths, conv_first, conv_second, gain_first, gain_second):
    slot_dev, rows, width, chans = latents.shape
    height = rows * lax.axis_size("tile")
    base = lax.axis_index("req") * slot_dev
    clip_here = clip_ids(base + jnp.arange(slot_dev, dtype=jnp.int32), lengths)
    clip_back = clip_ids(base - 2 + jnp.arange(slot_dev + 2, dtype=jnp.int32), lengths)
    member = (clip_here[:, None] == jnp.arange(lengths.shape[0], dtype=jnp.int32)[None, :]).astype(
        jnp.float32
    )
    causal = [(clip_back[dt : dt + slot_dev] == clip_here).astype(jnp.float32) for dt in range(3)]
    mean_one, rstd_one = group_stats(latents, member, lengths, height, width)
    act_first = activate(latents, mean_one, rstd_one, gain_first, 1.0)
    mid = causal_conv(row_faces(extend_frames(act_first)), conv_first, causal)
    mean_two, rstd_two = group_stats(mid, member, lengths, height, width)
    act_second = activate(mid, mean_two, rstd_two, gain_second, 1.0)
    final = causal_conv(row_faces(extend_frames(act_second)), conv_second, causal)
    return (latents.astype(jnp.float32) + final).astype(jnp.bfloat16)


def solution(mesh):
    return jax.shard_map(
        shards,
        mesh=mesh,
        in_specs=(P("req", "tile", None, None), P(), P(), P(), P(), P()),
        out_specs=P("req", "tile", None, None),
        check_vma=False,
    )
```

profile of v0, /device:TPU:1, one launch (start us, length us, event | category | flops | bytes accessed | tf_op | source)
XLA Modules:
  0.0 229.1 jit_solution(13481199546567014147)
XLA Ops:
  0.0 0.7 convert_multiply_fusion.1
  0.7 0.8 reduce-window.9
  1.5 0.7 bitcast_subtract_fusion
  2.3 1.3 convert_reduce_fusion
  4.3 69.4 %all-reduce.3 = (f32[4,32,16]{2,1,0:T(8,128)S(1)}, f32[4,32,16]{2,1,0:T(8,128)S(1)}) all-reduce(f32[4,32,16]{2,1,0:T(8,128)S(1)} %reshape.114, f32[4,32,16]{2,1,0:T(8,128)S(1)} %reshape.112), channel_id=1, replica_groups=mesh['req'=4,'tile'=32] {'req','tile'}, use_global_device_ids=true, to_apply=%region_7.8 | all-reduce | flops 4096 | bytes 32768 | tf_op jit(solution)/shard_map/psum | solution.py:40
  74.8 1.5 fusion.25
  76.3 2.0 collective-permute-start
  78.4 5.7 %fusion.54 = (bf16[1,3,3,512,512]{4,3,2,1,0:T(8,128)(2,1)S(1)}, bf16[1,3,3,512,512]{4,3,2,1,0:T(8,128)(2,1)S(1)}, bf16[1,3,3,512,512]{4,3,2,1,0:T(8,128)(2,1)S(1)}) fusion(bf16[3,3,3,512,512]{4,3,2,1,0:T(8,128)(2,1)} %param.8), kind=kLoop, calls=%fused_computation.118 | loop fusion | bytes 28311552 | tf_op jit(solution)/shard_map/slice | solution.py:85
  84.2 7.0 %collective-permute-done = bf16[2,4,80,512]{3,2,1,0:T(8,128)(2,1)S(1)} collective-permute-done((bf16[2,4,80,512]{3,2,1,0:T(8,128)(2,1)S(1)}, bf16[2,4,80,512]{3,2,1,0:T(8,128)(2,1)S(1)}, u32[]{:S(2)}, u32[]{:S(2)}) %collective-permute-start) | collective-permute-done | bytes 655392 | tf_op jit(solution)/shard_map/ppermute | solution.py:12
  91.2 3.7 %collective-permute-start.1 = (bf16[4,1,80,512]{3,2,1,0:T(8,128)(2,1)S(1)}, bf16[4,1,80,512]{3,2,1,0:T(8,128)(2,1)S(1)}, u32[]{:S(2)}, u32[]{:S(2)}) collective-permute-start(bf16[4,1,80,512]{3,2,1,0:T(8,128)(2,1)S(1)} %get-tuple-element.21), channel_id=1, source_target_pairs={{0,1},{1,2},{2,3},{3,4},{4,5},{5,6},{6,7},{7,8},{8,9},{9,10},{10,1... | collective-permute-start | bytes 983048 | tf_op jit(solution)/shard_map/ppermute | solution.py:20
  95.0 1.9 collective-permute-start.2
  97.0 2.0 collective-permute-done.1
  99.0 4.4 %collective-permute-done.2 = bf16[4,1,80,512]{3,2,1,0:T(8,128)(2,1)S(1)} collective-permute-done((bf16[4,1,80,512]{3,2,1,0:T(8,128)(2,1)S(1)}, bf16[4,1,80,512]{3,2,1,0:T(8,128)(2,1)S(1)}, u32[]{:S(2)}, u32[]{:S(2)}) %collective-permute-start.2) | collective-permute-done | bytes 327712 | tf_op jit(solution)/shard_map/ppermute | solution.py:23
  103.4 1.3 fusion.8
  105.6 0.5 slice_dynamic-update-slice_fusion.8
  106.4 0.5 slice_dynamic-update-slice_fusion.6
  106.8 3.2 %convolution_multiply_fusion.3 = f32[2,4,80,512]{3,2,1,0:T(8,128)S(1)} fusion(bf16[4,4,80,4608]{3,2,1,0:T(8,128)(2,1)S(1)} %slice_dynamic-update-slice_fusion.6, bf16[4608,512,1,1]{1,0,3,2:T(8,128)(2,1)S(1)} %bitcast.55, f32[2]{0:T(128)S(1)} %get-tuple-element.28), kind=kOutput, calls=%fused_computation.32 | convolution fusion | flops 3020226560 | bytes 17825800 | tf_op jit(solution)/shard_map/dot_general | solution.py:85
  110.0 3.2 %convolution_multiply_fusion.4 = f32[2,4,80,512]{3,2,1,0:T(8,128)S(1)} fusion(bf16[4,4,80,4608]{3,2,1,0:T(8,128)(2,1)S(1)} %slice_dynamic-update-slice_fusion.6, bf16[4608,512,1,1]{1,0,3,2:T(8,128)(2,1)S(1)} %bitcast.54, f32[2]{0:T(128)S(1)} %get-tuple-element.29), kind=kOutput, calls=%fused_computation.33 | convolution fusion | flops 3020226560 | bytes 17825800 | tf_op jit(solution)/shard_map/dot_general | solution.py:85
  113.3 3.4 %fusion.52 = (f32[2,512]{1,0:T(2,128)S(1)}, f32[2,512]{1,0:T(2,128)S(1)}, f32[2,4,80,512]{3,2,1,0:T(8,128)S(1)}) fusion(f32[2,4,80,512]{3,2,1,0:T(8,128)S(1)} %convolution_multiply_fusion.3, f32[2,4,80,512]{3,2,1,0:T(8,128)S(1)} %convolution_multiply_fusion.4, bf16[4,4,80,4608]{3,2,1,0:T(8,128)(2,1)S(1)} %slice_dynamic-update-slice_fusion.6, ...), kind=kOutput, calls=%fused_computation.116 | convolution fusion | flops 3021862912 | bytes 20455432 | tf_op jit(solution)/shard_map/dot_general | solution.py:85
  117.3 68.3 %all-reduce.2 = (f32[4,32,16]{2,1,0:T(8,128)S(1)}, f32[4,32,16]{2,1,0:T(8,128)S(1)}) all-reduce(f32[4,32,16]{2,1,0:T(8,128)S(1)} %reshape.118, f32[4,32,16]{2,1,0:T(8,128)S(1)} %reshape.116), channel_id=1, replica_groups=mesh['req'=4,'tile'=32] {'req','tile'}, use_global_device_ids=true, to_apply=%region_13.14 | all-reduce | flops 4096 | bytes 32768 | tf_op jit(solution)/shard_map/psum | solution.py:40
  187.1 3.0 %collective-permute-start.3 = (bf16[2,4,80,512]{3,2,1,0:T(8,128)(2,1)S(1)}, bf16[2,4,80,512]{3,2,1,0:T(8,128)(2,1)S(1)}, u32[]{:S(2)}, u32[]{:S(2)}) collective-permute-start(bf16[2,4,80,512]{3,2,1,0:T(8,128)(2,1)S(1)} %multiply_convert_fusion), channel_id=1, source_target_pairs={{0,32},{32,64},{64,96},{1,33},{33,65},{65,97},{2,34},{34,66},{66,9... | collective-permute-start | bytes 1966088 | tf_op jit(solution)/shard_map/ppermute | solution.py:12
  190.1 13.1 %collective-permute-done.3 = bf16[2,4,80,512]{3,2,1,0:T(8,128)(2,1)S(1)} collective-permute-done((bf16[2,4,80,512]{3,2,1,0:T(8,128)(2,1)S(1)}, bf16[2,4,80,512]{3,2,1,0:T(8,128)(2,1)S(1)}, u32[]{:S(2)}, u32[]{:S(2)}) %collective-permute-start.3) | collective-permute-done | bytes 655392 | tf_op jit(solution)/shard_map/ppermute | solution.py:12
  203.3 3.4 %collective-permute-start.4 = (bf16[4,1,80,512]{3,2,1,0:T(8,128)(2,1)S(1)}, bf16[4,1,80,512]{3,2,1,0:T(8,128)(2,1)S(1)}, u32[]{:S(2)}, u32[]{:S(2)}) collective-permute-start(bf16[4,1,80,512]{3,2,1,0:T(8,128)(2,1)S(1)} %get-tuple-element.19), channel_id=1, source_target_pairs={{0,1},{1,2},{2,3},{3,4},{4,5},{5,6},{6,7},{7,8},{8,9},{9,10},{10,1... | collective-permute-start | bytes 983048 | tf_op jit(solution)/shard_map/ppermute | solution.py:20
  206.7 1.9 collective-permute-start.5
  208.6 5.7 %fusion.53 = (bf16[1,3,3,512,512]{4,3,2,1,0:T(8,128)(2,1)S(1)}, bf16[1,3,3,512,512]{4,3,2,1,0:T(8,128)(2,1)S(1)}, bf16[1,3,3,512,512]{4,3,2,1,0:T(8,128)(2,1)S(1)}) fusion(bf16[3,3,3,512,512]{4,3,2,1,0:T(8,128)(2,1)} %param.9), kind=kLoop, calls=%fused_computation.117 | loop fusion | bytes 28311552 | tf_op jit(solution)/shard_map/slice | solution.py:85
  214.4 0.7 collective-permute-done.5
  215.1 1.3 select_maximum_fusion
  217.3 0.5 slice_dynamic-update-slice_fusion.2
  218.1 0.5 slice_dynamic-update-slice_fusion
  218.6 3.2 %convolution_multiply_fusion = f32[2,4,80,512]{3,2,1,0:T(8,128)S(1)} fusion(bf16[4,4,80,4608]{3,2,1,0:T(8,128)(2,1)S(1)} %slice_dynamic-update-slice_fusion, bf16[4608,512,1,1]{1,0,3,2:T(8,128)(2,1)S(1)} %bitcast.58, f32[2]{0:T(128)S(1)} %get-tuple-element.28), kind=kOutput, calls=%fused_computation.29 | convolution fusion | flops 3020226560 | bytes 17825800 | tf_op jit(solution)/shard_map/dot_general | solution.py:85
  221.8 3.2 %convolution_multiply_fusion.1 = f32[2,4,80,512]{3,2,1,0:T(8,128)S(1)} fusion(bf16[4,4,80,4608]{3,2,1,0:T(8,128)(2,1)S(1)} %slice_dynamic-update-slice_fusion, bf16[4608,512,1,1]{1,0,3,2:T(8,128)(2,1)S(1)} %bitcast.57, f32[2]{0:T(128)S(1)} %get-tuple-element.29), kind=kOutput, calls=%fused_computation.30 | convolution fusion | flops 3020226560 | bytes 17825800 | tf_op jit(solution)/shard_map/dot_general | solution.py:85
  225.0 4.1 %fusion.15 = bf16[2,4,80,512]{3,2,1,0:T(8,128)(2,1)} fusion(f32[2,4,80,512]{3,2,1,0:T(8,128)S(1)} %convolution_multiply_fusion, f32[2,4,80,512]{3,2,1,0:T(8,128)S(1)} %convolution_multiply_fusion.1, bf16[4,4,80,4608]{3,2,1,0:T(8,128)(2,1)S(1)} %slice_dynamic-update-slice_fusion, bf16[4608,512,1,1]{1,0,3,2:T(8,128)(2,1)S(1)} %bitcast.56, ...), kind=kOutput, calls=%fused_computation.39 | convolution fusion | flops 3021864960 | bytes 20447240 | tf_op jit(solution)/shard_map/dot_general | solution.py:85
  (54 shorter events, 6.8 us)
Async XLA Ops:
  76.3 14.9 %collective-permute-start = (bf16[2,4,80,512]{3,2,1,0:T(8,128)(2,1)S(1)}, bf16[2,4,80,512]{3,2,1,0:T(8,128)(2,1)S(1)}, u32[]{:S(2)}, u32[]{:S(2)}) collective-permute-start(bf16[2,4,80,512]{3,2,1,0:T(8,128)(2,1)S(1)} %fusion.25), channel_id=1, source_target_pairs={{0,32},{32,64},{64,96},{1,33},{33,65},{65,97},{2,34},{34,66},{66,9... | collective-permute-start | bytes 1966088 | tf_op jit(solution)/shard_map/ppermute | solution.py:12
  91.2 7.7 %collective-permute-start.1 = (bf16[4,1,80,512]{3,2,1,0:T(8,128)(2,1)S(1)}, bf16[4,1,80,512]{3,2,1,0:T(8,128)(2,1)S(1)}, u32[]{:S(2)}, u32[]{:S(2)}) collective-permute-start(bf16[4,1,80,512]{3,2,1,0:T(8,128)(2,1)S(1)} %get-tuple-element.21), channel_id=1, source_target_pairs={{0,1},{1,2},{2,3},{3,4},{4,5},{5,6},{6,7},{7,8},{8,9},{9,10},{10,1... | collective-permute-start | bytes 983048 | tf_op jit(solution)/shard_map/ppermute | solution.py:20
  95.0 8.4 %collective-permute-start.2 = (bf16[4,1,80,512]{3,2,1,0:T(8,128)(2,1)S(1)}, bf16[4,1,80,512]{3,2,1,0:T(8,128)(2,1)S(1)}, u32[]{:S(2)}, u32[]{:S(2)}) collective-permute-start(bf16[4,1,80,512]{3,2,1,0:T(8,128)(2,1)S(1)} %get-tuple-element.22), channel_id=1, source_target_pairs={{1,0},{2,1},{3,2},{4,3},{5,4},{6,5},{7,6},{8,7},{9,8},{10,9},{11,1... | collective-permute-start | bytes 983048 | tf_op jit(solution)/shard_map/ppermute | solution.py:23
  113.2 73.5 %copy-start.1 = (f32[512]{0:T(512)S(1)}, f32[512]{0:T(512)}, u32[]{:S(2)}) copy-start(f32[512]{0:T(512)} %param.11) | copy-start | bytes 6148
  187.1 16.1 %collective-permute-start.3 = (bf16[2,4,80,512]{3,2,1,0:T(8,128)(2,1)S(1)}, bf16[2,4,80,512]{3,2,1,0:T(8,128)(2,1)S(1)}, u32[]{:S(2)}, u32[]{:S(2)}) collective-permute-start(bf16[2,4,80,512]{3,2,1,0:T(8,128)(2,1)S(1)} %multiply_convert_fusion), channel_id=1, source_target_pairs={{0,32},{32,64},{64,96},{1,33},{33,65},{65,97},{2,34},{34,66},{66,9... | collective-permute-start | bytes 1966088 | tf_op jit(solution)/shard_map/ppermute | solution.py:12
  203.3 11.1 %collective-permute-start.4 = (bf16[4,1,80,512]{3,2,1,0:T(8,128)(2,1)S(1)}, bf16[4,1,80,512]{3,2,1,0:T(8,128)(2,1)S(1)}, u32[]{:S(2)}, u32[]{:S(2)}) collective-permute-start(bf16[4,1,80,512]{3,2,1,0:T(8,128)(2,1)S(1)} %get-tuple-element.19), channel_id=1, source_target_pairs={{0,1},{1,2},{2,3},{3,4},{4,5},{5,6},{6,7},{7,8},{8,9},{9,10},{10,1... | collective-permute-start | bytes 983048 | tf_op jit(solution)/shard_map/ppermute | solution.py:20
  206.7 8.4 %collective-permute-start.5 = (bf16[4,1,80,512]{3,2,1,0:T(8,128)(2,1)S(1)}, bf16[4,1,80,512]{3,2,1,0:T(8,128)(2,1)S(1)}, u32[]{:S(2)}, u32[]{:S(2)}) collective-permute-start(bf16[4,1,80,512]{3,2,1,0:T(8,128)(2,1)S(1)} %get-tuple-element.20), channel_id=1, source_target_pairs={{1,0},{2,1},{3,2},{4,3},{5,4},{6,5},{7,6},{8,7},{9,8},{10,9},{11,1... | collective-permute-start | bytes 983048 | tf_op jit(solution)/shard_map/ppermute | solution.py:23
  221.8 3.2 %copy-start = (bf16[2,4,80,512]{3,2,1,0:T(8,128)(2,1)S(1)}, bf16[2,4,80,512]{3,2,1,0:T(8,128)(2,1)}, u32[]{:S(2)}) copy-start(bf16[2,4,80,512]{3,2,1,0:T(8,128)(2,1)} %param.6) | copy-start | bytes 1966084
where the time goes:
time: 232 us; the launch traced here: 229 us
  blocking collectives  138 us (59%)
  waiting for transfers between devices  27.2 us (12%)
  matrix products  22.1 us (10%)
  local copies, waits for them, and re-layouts  16.2 us (7%)
  starting transfers between devices  16 us (7%)
  other arithmetic  9.61 us (4%)
    psum x2, blocking collectives, group_stats(): lax.psum((clip_total, clip_squares), ('req', 'tile'))  138 us
    dot_general x6, matrix products, causal_conv(): jnp.dot(block, taps[dt], preferred_element_type=jnp.float32)  20.3 us
    ppermute x2, waiting for transfers between devices, passed_along(): return lax.ppermute(block, axis, route)  20.1 us
    slice x2, local copies, waits for them, and re-layouts, causal_conv(): taps[dt]  11.5 us
    ppermute x2, starting transfers between devices, with_halo(): lax.ppermute(lax.slice_in_dim(block, block.shape[dim] - width, None, axis...  7.19 us
    ppermute x2, waiting for transfers between devices, with_halo(): lax.ppermute(lax.slice_in_dim(block, 0, width, axis=dim), axis, backward)  5.1 us
    ppermute x2, starting transfers between devices, passed_along(): return lax.ppermute(block, axis, route)  4.95 us
  transfers between devices with their start and end apart: 6, of which 5 were waited for; matrix products, arithmetic and copies ran while one was open for 5% of the time, Pallas kernels for 0%

commit v1 on v0

v1 whole, which is shorter than its diff:
```python
import functools

import jax
import jax.numpy as jnp
from jax import lax
from jax.experimental import pallas as pl
from jax.experimental.pallas import tpu as pltpu
from jax.sharding import PartitionSpec as P

GROUPS = 32
MESH = pl.DeviceIdType.MESH
F32 = jnp.float32
BF16 = jnp.bfloat16
NX, NY, NZ, NC = 4, 4, 4, 2
NT = NZ * NY * NC


def lane_ids(shape):
    return lax.broadcasted_iota(jnp.int32, shape, 1)


def swap_lanes(x, step):
    lanes = lane_ids(x.shape)
    return jnp.where((lanes & step) != 0, pltpu.roll(x, step, 1), pltpu.roll(x, 128 - step, 1))


def segment_sum(x):
    for step in (1, 2, 4, 8):
        x = x + swap_lanes(x, step)
    return x


def block_kernel(
    lengths, lat, w1_hbm, w2_hbm, gain1, gain2, out,
    w1, w2, x_raw, m_raw, act, acc, mid, stage, rows_scr, e_scr, p_scr, mean_scr, scale_scr,
    src1, buf1, src2, buf2, send_sem, recv_sem, local_sem,
):
    r = lax.axis_index("req")
    t = lax.axis_index("tile")
    cells = lat.shape[1] * lat.shape[2]
    width = lat.shape[2]
    z = t // (NY * NC)
    yc = lax.rem(t, NY * NC)
    right = (lax.rem(r + 1, NX), t)
    above = (r, lax.rem(t + NT - 1, NT))
    below = (r, lax.rem(t + 1, NT))
    peers1 = [(r, z * (NY * NC) + lax.rem(yc + j, NY * NC)) for j in range(1, NY * NC)]
    peers2 = [
        (lax.rem(r + j // NZ, NX), lax.rem(t + (NY * NC) * (j % NZ), NT)) for j in range(1, NX * NZ)
    ]

    barrier = pltpu.get_barrier_semaphore()
    greeted = peers1 + peers2 + [above, below]
    for peer in greeted:
        pl.semaphore_signal(barrier, inc=1, device_id=peer, device_id_type=MESH)

    lat_copy = pltpu.make_async_copy(lat, x_raw.at[2:4, 1:5], local_sem.at[0])
    lat_copy.start()
    w_copies = [
        pltpu.make_async_copy(w1_hbm, w1, local_sem.at[1]),
        pltpu.make_async_copy(w2_hbm, w2, local_sem.at[2]),
    ]
    for copy in w_copies:
        copy.start()

    used = [0]
    sent = []

    def send(src, dst, peer):
        i = used[0]
        used[0] += 1
        copy = pltpu.make_async_remote_copy(
            src_ref=src, dst_ref=dst, send_sem=send_sem.at[i], recv_sem=recv_sem.at[i],
            device_id=peer, device_id_type=MESH,
        )
        copy.start()
        sent.append(copy)
        return copy

    first = lengths[0]
    second = first + lengths[1]
    third = second + lengths[2]

    def one(condition):
        return jnp.where(condition, 1, 0)

    def clip(s):
        return one(s >= 0) + one(s >= first) + one(s >= second) + one(s >= third) - 1

    base = 2 * r
    clip_q = [clip(base - 2 + q) for q in range(4)]

    def same(a, b):
        return jnp.where(a == b, 1.0, 0.0).astype(F32)

    pair = {
        (0, 0): same(clip_q[0], clip_q[2]),
        (1, 0): same(clip_q[1], clip_q[2]),
        (0, 1): same(clip_q[1], clip_q[3]),
        (1, 1): same(clip_q[2], clip_q[3]),
    }

    def pack(use):
        sums = segment_sum(rows_scr[...])
        row = lax.broadcasted_iota(jnp.int32, (16, 128), 0)
        picked = jnp.where((lane_ids((16, 128)) & 15) == row, sums, 0.0)
        src1[use] = jnp.broadcast_to(jnp.sum(picked, axis=0, keepdims=True), (8, 128))

    def put_rows(frame, total, squares):
        for kind, value in enumerate((total, squares)):
            value = jnp.sum(value, axis=0, keepdims=True)
            for b in range(4):
                k = 4 * (2 * frame + kind) + b
                rows_scr[k : k + 1, :] = value[:, b * 128 : (b + 1) * 128]

    def exchange_one(use):
        return [send(src1.at[use], buf1.at[use, j], peer) for j, peer in enumerate(peers1)]

    def exchange_two(use, copies):
        for copy in copies:
            copy.wait_recv()
        total = src1[use]
        for j in range(len(peers1)):
            total = total + buf1[use, j]
        src2[use] = total
        return [send(src2.at[use], buf2.at[use, j], peer) for j, peer in enumerate(peers2)]

    def params(use, copies, gain):
        for copy in copies:
            copy.wait_recv()
        lanes = lane_ids((8, 128))
        parts = []
        for dx in range(NX):
            total = src2[use] if dx == 0 else buf2[use, NZ * dx - 1]
            for dz in range(1, NZ):
                total = total + buf2[use, NZ * dx + dz - 1]
            parts.append(total)
        row8 = lax.broadcasted_iota(jnp.int32, (8, 128), 0)
        early = (lanes & 8) == 0
        for q in range(4):
            mixed = jnp.zeros((8, 128), F32)
            count = jnp.float32(0.0)
            for dx in range(NX):
                rr = lax.rem(r + NX - dx, NX)
                m0 = same(clip(2 * rr), clip_q[q])
                m1 = same(clip(2 * rr + 1), clip_q[q])
                count = count + m0 + m1
                mixed = mixed + jnp.where(early, m0, m1) * parts[dx]
            mixed = mixed + swap_lanes(mixed, 8)
            e_scr[8 * q : 8 * q + 8] = jnp.where((lanes & 15) == row8, mixed, 0.0)
            p_scr[8 * q : 8 * q + 8] = jnp.full((8, 128), jnp.maximum(count, 1.0), F32)
        e_scr[...] = segment_sum(e_scr[...]) / (p_scr[...] * float(128 * 80 * 512 // GROUPS))
        for q in range(4):
            mean = e_scr[8 * q : 8 * q + 4]
            scale = lax.rsqrt(e_scr[8 * q + 4 : 8 * q + 8] - mean * mean + 1e-06) * gain[...]
            p_scr[4 * q : 4 * q + 4] = scale
        for q in range(4):
            for b in range(4):
                mean_scr[q : q + 1, b * 128 : (b + 1) * 128] = e_scr[8 * q + b : 8 * q + b + 1, :]
                scale_scr[q : q + 1, b * 128 : (b + 1) * 128] = p_scr[4 * q + b : 4 * q + b + 1, :]

    def activated(value, q):
        v = (value - mean_scr[q : q + 1, :]) * scale_scr[q : q + 1, :]
        half = 0.5 * v
        return half + half * jnp.tanh(half)

    def place(value, q, row):
        if q == 3:
            act[2, 1, row] = value.astype(BF16)
        elif q == 2:
            act[2, 0, row] = value.astype(BF16)
            act[1, 1, row] = (value * pair[1, 1]).astype(BF16)
        elif q == 1:
            act[1, 0, row] = (value * pair[1, 0]).astype(BF16)
            act[0, 1, row] = (value * pair[0, 1]).astype(BF16)
        else:
            act[0, 0, row] = (value * pair[0, 0]).astype(BF16)

    def inside(row):
        out_top = one(row == 0) * one(t == 0)
        out_bottom = one(row == 5) * one(t == NT - 1)
        return (1 - out_top - out_bottom).astype(F32)

    def activate_rows(raw, q):
        @pl.loop(0, 6)
        def _(row):
            place(activated(raw[q, row].astype(F32), q) * inside(row), q, row)

    def activate_wide(q):
        @pl.loop(0, 4)
        def _(row):
            place(activated(mid[q - 2, row], q), q, row + 1)

        for row in (0, 5):
            place(activated(m_raw[q, row].astype(F32), q) * inside(row), q, row)

    def conv_step(w, frame, dx):
        lhs = jnp.concatenate(
            [act[dt, frame, dy : dy + 4].reshape(cells, 512) for dt in range(3) for dy in range(3)],
            axis=-1,
        )
        for n in range(2):
            cols = slice(n * 256, (n + 1) * 256)
            rhs = jnp.concatenate(
                [w[dt, dy, dx, :, cols] for dt in range(3) for dy in range(3)], axis=0
            )
            acc[dx, :, cols] = jnp.dot(lhs, rhs, preferred_element_type=F32)

    def conv(w, frame, start, stop):
        @pl.loop(start, stop)
        def _(dx):
            conv_step(w, frame, dx)

    def conv_row(row):
        rows = pl.ds(pl.multiple_of(row * width, 16), width)
        column = lax.broadcasted_iota(jnp.int32, (width, 512), 0)
        low = jnp.where(column == 0, 0.0, pltpu.roll(acc[0, rows, :], 1, 0))
        high = jnp.where(column == width - 1, 0.0, pltpu.roll(acc[2, rows, :], width - 1, 0))
        return acc[1, rows, :] + low + high

    def sums_of(value):
        parts = value.reshape(width // 8, 8, 512)
        return jnp.sum(parts, axis=0), jnp.sum(parts * parts, axis=0)

    zero = jnp.zeros((8, 512), F32)

    lat_copy.wait()
    for frame in range(2):
        def latent_row(row, carry, frame=frame):
            total, squares = sums_of(x_raw[2 + frame, row + 1].astype(F32))
            return carry[0] + total, carry[1] + squares

        put_rows(frame, *lax.fori_loop(0, 4, latent_row, (zero, zero)))
    pack(0)
    pl.semaphore_wait(barrier, len(greeted))

    def send_frame(src_rows, dst, frame):
        edges = [send(src_rows(frame, row, 1), dst.at[frame, row + 1 : row + 2], right) for row in (0, 3)]
        inner = send(src_rows(frame, 1, 2), dst.at[frame, 2:4], right)
        return edges, inner

    def pass_edges(dst, q, edges):
        for edge in edges:
            edge.wait_recv()
        return [
            send(dst.at[q, 1:2], dst.at[q, 5:6], above),
            send(dst.at[q, 4:5], dst.at[q, 0:1], below),
        ]

    stats = exchange_one(0)

    def lat_rows(frame, row, n):
        return lat.at[frame, row : row + n]

    edges1, inner1 = send_frame(lat_rows, x_raw, 1)
    faces = [
        send(lat.at[0:2, 0:1], x_raw.at[2:4, 5:6], above),
        send(lat.at[0:2, 3:4], x_raw.at[2:4, 0:1], below),
    ]
    edges0, inner0 = send_frame(lat_rows, x_raw, 0)
    stats = exchange_two(0, stats)
    passed1 = pass_edges(x_raw, 1, edges1)
    params(0, stats, gain1)
    for copy in faces:
        copy.wait_recv()
    activate_rows(x_raw, 3)
    activate_rows(x_raw, 2)
    inner1.wait_recv()
    for copy in passed1:
        copy.wait_recv()
    activate_rows(x_raw, 1)
    w_copies[0].wait()
    conv(w1, 1, 0, 2)
    passed0 = pass_edges(x_raw, 0, edges0)
    conv(w1, 1, 2, 3)

    def finish_mid(frame):
        def mid_row(row, carry):
            value = conv_row(row)
            mid[frame, row] = value
            m_raw[2 + frame, row + 1] = value.astype(BF16)
            total, squares = sums_of(value)
            return carry[0] + total, carry[1] + squares

        put_rows(frame, *lax.fori_loop(0, 4, mid_row, (zero, zero)))

    def mid_rows(frame, row, n):
        return m_raw.at[2 + frame, row + 1 : row + 1 + n]

    def mid_faces(frame):
        return [
            send(m_raw.at[2 + frame, 1:2], m_raw.at[2 + frame, 5:6], above),
            send(m_raw.at[2 + frame, 4:5], m_raw.at[2 + frame, 0:1], below),
        ]

    finish_mid(1)
    edges1, inner1b = send_frame(mid_rows, m_raw, 1)
    faces = mid_faces(1)
    inner0.wait_recv()
    for copy in passed0:
        copy.wait_recv()
    activate_rows(x_raw, 0)
    conv(w1, 0, 0, 3)
    finish_mid(0)
    pack(1)
    stats = exchange_one(1)
    faces += mid_faces(0)
    edges0, inner0b = send_frame(mid_rows, m_raw, 0)
    passed1 = pass_edges(m_raw, 1, edges1)
    stats = exchange_two(1, stats)
    params(1, stats, gain2)
    for copy in faces:
        copy.wait_recv()
    activate_wide(3)
    activate_wide(2)
    inner1b.wait_recv()
    for copy in passed1:
        copy.wait_recv()
    activate_rows(m_raw, 1)
    w_copies[1].wait()
    passed0 = pass_edges(m_raw, 0, edges0)
    conv(w2, 1, 0, 3)

    def finish_out(frame):
        @pl.loop(0, 4)
        def _(row):
            stage[frame, row] = (x_raw[2 + frame, row + 1].astype(F32) + conv_row(row)).astype(BF16)

        copy = pltpu.make_async_copy(stage.at[frame], out.at[frame], local_sem.at[3 + frame])
        copy.start()
        return copy

    out1 = finish_out(1)
    inner0b.wait_recv()
    for copy in passed0:
        copy.wait_recv()
    activate_rows(m_raw, 0)
    conv(w2, 0, 0, 3)
    out0 = finish_out(0)
    for copy in sent:
        copy.wait_send()
    out1.wait()
    out0.wait()


N_SENDS = 2 * (NY * NC - 1) + 2 * (NX * NZ - 1) + 12 + 6 + 8


def shards(latents, lengths, conv_first, conv_second, gain_first, gain_second):
    frames, rows, width, chans = latents.shape
    smem = pl.BlockSpec(memory_space=pltpu.SMEM)
    vmem = pl.BlockSpec(memory_space=pltpu.VMEM)
    hbm = pl.BlockSpec(memory_space=pl.ANY)
    flops = 2 * 2 * frames * rows * width * 27 * chans * chans
    return pl.pallas_call(
        block_kernel,
        out_shape=jax.ShapeDtypeStruct(latents.shape, latents.dtype),
        in_specs=[smem, hbm, hbm, hbm, vmem, vmem],
        out_specs=hbm,
        scratch_shapes=[
            pltpu.VMEM(conv_first.shape, BF16),
            pltpu.VMEM(conv_second.shape, BF16),
            pltpu.VMEM((4, rows + 2, width, chans), BF16),
            pltpu.VMEM((4, rows + 2, width, chans), BF16),
            pltpu.VMEM((3, 2, rows + 2, width, chans), BF16),
            pltpu.VMEM((3, rows * width, chans), F32),
            pltpu.VMEM((2, rows, width, chans), F32),
            pltpu.VMEM((2, rows, width, chans), BF16),
            pltpu.VMEM((16, 128), F32),
            pltpu.VMEM((32, 128), F32),
            pltpu.VMEM((32, 128), F32),
            pltpu.VMEM((8, chans), F32),
            pltpu.VMEM((8, chans), F32),
            pltpu.VMEM((2, 8, 128), F32),
            pltpu.VMEM((2, NY * NC - 1, 8, 128), F32),
            pltpu.VMEM((2, 8, 128), F32),
            pltpu.VMEM((2, NX * NZ - 1, 8, 128), F32),
            pltpu.SemaphoreType.DMA((N_SENDS,)),
            pltpu.SemaphoreType.DMA((N_SENDS,)),
            pltpu.SemaphoreType.DMA((5,)),
        ],
        compiler_params=pltpu.CompilerParams(
            collective_id=0, has_side_effects=True, vmem_limit_bytes=60 * 2**20
        ),
        cost_estimate=pl.CostEstimate(
            flops=flops, bytes_accessed=2 * conv_first.size * 2 + 2 * latents.size * 2, transcendentals=latents.size * 6
        ),
    )(
        lengths, latents, conv_first, conv_second,
        gain_first.reshape(4, chans // 4), gain_second.reshape(4, chans // 4),
    )


def solution(mesh):
    return jax.shard_map(
        shards,
        mesh=mesh,
        in_specs=(P("req", "tile", None, None), P(), P(), P(), P(), P()),
        out_specs=P("req", "tile", None, None),
        check_vma=False,
    )
```

time: 232 us -> 69.5 us (0.30); the launches traced: 229 us -> 69.3 us
  blocking collectives: 138 us -> 0 us
  Pallas kernels: 0 us -> 67.4 us
  waiting for transfers between devices: 27.2 us -> 0 us
  matrix products: 22.1 us -> 0 us
  starting transfers between devices: 16 us -> 0 us
  local copies, waits for them, and re-layouts: 16.2 us -> 1.97 us
  other arithmetic: 9.61 us -> 0 us
    psum x2 -> x0, blocking collectives: 138 us -> none  [group_stats(): lax.psum((clip_total, clip_squares), ('req', 'tile'))]
    pallas_call x0 -> x1, Pallas kernels: none -> 67.4 us  [shards(): pl.pallas_call(block_kernel, out_shape=jax.ShapeDtypeStruct(latents.shape...]
    ppermute x6 -> x0, waiting for transfers between devices: 27.2 us -> none  [the longest x2 20.1 us: passed_along(): return lax.ppermute(block, axis, route)]
    dot_general x14 -> x0, matrix products: 22.1 us -> none  [the longest x6 20.3 us: causal_conv(): jnp.dot(block, taps[dt], preferred_element_type=jnp.float32)]
    ppermute x6 -> x0, starting transfers between devices: 16 us -> none  [the longest x2 7.19 us: with_halo(): lax.ppermute(lax.slice_in_dim(block, block.shape[dim] - width, None, axis...]
    slice x2 -> x0, local copies, waits for them, and re-layouts: 11.5 us -> none  [causal_conv(): taps[dt]]
    concatenate x4 -> x0, other arithmetic: 2.62 us -> none  [the longest x2 2.5 us: with_halo(): block = jnp.concatenate([low, block, high], axis=dim)]
  transfers between devices with their start and end apart: 6 -> 0, of which waited for: 5 -> 0; matrix products, arithmetic and copies ran while one was open for 5% -> 0% of each run, Pallas kernels for 0% -> 0%
where the time goes in v1:
time: 69.5 us; the launch traced here: 69.3 us
  Pallas kernels  67.4 us (97%)
  local copies, waits for them, and re-layouts  1.97 us (3%)
    pallas_call x1, Pallas kernels, shards(): pl.pallas_call(block_kernel, out_shape=jax.ShapeDtypeStruct(latents.shape...  67.4 us
    unnamed x1, local copies, waits for them, and re-layouts  1.97 us

profile of v1, /device:TPU:1, one launch (start us, length us, event | category | flops | bytes accessed | tf_op | source)
XLA Modules:
  0.0 69.3 jit_solution(12209922746771999440)
XLA Ops:
  0.0 67.4 %shard_map.64 = bf16[2,4,80,512]{3,2,1,0:T(8,128)(2,1)} custom-call(s32[4]{0:T(128)} %lengths.1, bf16[2,4,80,512]{3,2,1,0:T(8,128)(2,1)} %lat.1, bf16[3,3,3,512,512]{4,3,2,1,0:T(8,128)(2,1)} %w1_hbm.1, bf16[3,3,3,512,512]{4,3,2,1,0:T(8,128)(2,1)} %w2_hbm.1, f32[4,128]{1,0:T(4,128)} %bitcast.2, f32[4,128]{1,0:T(4,128)} %bitcast.3), custom_call_target="tpu_custom_call" | custom-call | flops 18119393280 | bytes 29622272 | tf_op jit(solution)/shard_map/pallas_call | solution.py:355
  67.4 2.0 %copy.8 = bf16[2,4,80,512]{3,2,1,0:T(8,128)(2,1)} copy(bf16[2,4,80,512]{3,2,1,0:T(8,128)(2,1)} %shard_map.64) | data formatting | bytes 1310720

commit v2 on v1

--- a/solution.py
+++ b/solution.py
@@ -44,10 +44,10 @@
     right = (lax.rem(r + 1, NX), t)
     above = (r, lax.rem(t + NT - 1, NT))
     below = (r, lax.rem(t + 1, NT))
-    peers1 = [(r, z * (NY * NC) + lax.rem(yc + j, NY * NC)) for j in range(1, NY * NC)]
-    peers2 = [
+    peers1 = [
         (lax.rem(r + j // NZ, NX), lax.rem(t + (NY * NC) * (j % NZ), NT)) for j in range(1, NX * NZ)
     ]
+    peers2 = [(r, z * (NY * NC) + lax.rem(yc + j, NY * NC)) for j in range(1, NY * NC)]
 
     barrier = pltpu.get_barrier_semaphore()
     greeted = peers1 + peers2 + [above, below]
@@ -119,22 +119,24 @@
     def exchange_two(use, copies):
         for copy in copies:
             copy.wait_recv()
-        total = src1[use]
-        for j in range(len(peers1)):
-            total = total + buf1[use, j]
-        src2[use] = total
+        row8 = lax.broadcasted_iota(jnp.int32, (8, 128), 0)
+        rows = jnp.zeros((8, 128), F32)
+        for dx in range(NX):
+            total = src1[use] if dx == 0 else buf1[use, NZ * dx - 1]
+            for dz in range(1, NZ):
+                total = total + buf1[use, NZ * dx + dz - 1]
+            rows = rows + jnp.where(row8 == dx, total, 0.0)
+        src2[use] = rows
         return [send(src2.at[use], buf2.at[use, j], peer) for j, peer in enumerate(peers2)]
 
     def params(use, copies, gain):
         for copy in copies:
             copy.wait_recv()
         lanes = lane_ids((8, 128))
-        parts = []
-        for dx in range(NX):
-            total = src2[use] if dx == 0 else buf2[use, NZ * dx - 1]
-            for dz in range(1, NZ):
-                total = total + buf2[use, NZ * dx + dz - 1]
-            parts.append(total)
+        total = src2[use]
+        for j in range(len(peers2)):
+            total = total + buf2[use, j]
+        parts = [jnp.broadcast_to(total[dx : dx + 1], (8, 128)) for dx in range(NX)]
         row8 = lax.broadcasted_iota(jnp.int32, (8, 128), 0)
         early = (lanes & 8) == 0
         for q in range(4):
@@ -234,10 +236,11 @@
     pack(0)
     pl.semaphore_wait(barrier, len(greeted))
 
-    def send_frame(src_rows, dst, frame):
-        edges = [send(src_rows(frame, row, 1), dst.at[frame, row + 1 : row + 2], right) for row in (0, 3)]
-        inner = send(src_rows(frame, 1, 2), dst.at[frame, 2:4], right)
-        return edges, inner
+    def send_edges(src_rows, dst, frame):
+        return [send(src_rows(frame, row, 1), dst.at[frame, row + 1 : row + 2], right) for row in (0, 3)]
+
+    def send_inner(src_rows, dst, frame):
+        return send(src_rows(frame, 1, 2), dst.at[frame, 2:4], right)
 
     def pass_edges(dst, q, edges):
         for edge in edges:
@@ -252,12 +255,14 @@
     def lat_rows(frame, row, n):
         return lat.at[frame, row : row + n]
 
-    edges1, inner1 = send_frame(lat_rows, x_raw, 1)
+    edges1 = send_edges(lat_rows, x_raw, 1)
+    inner1 = send_inner(lat_rows, x_raw, 1)
     faces = [
         send(lat.at[0:2, 0:1], x_raw.at[2:4, 5:6], above),
         send(lat.at[0:2, 3:4], x_raw.at[2:4, 0:1], below),
     ]
-    edges0, inner0 = send_frame(lat_rows, x_raw, 0)
+    edges0 = send_edges(lat_rows, x_raw, 0)
+    inner0 = send_inner(lat_rows, x_raw, 0)
     stats = exchange_two(0, stats)
     passed1 = pass_edges(x_raw, 1, edges1)
     params(0, stats, gain1)
@@ -294,7 +299,7 @@
         ]
 
     finish_mid(1)
-    edges1, inner1b = send_frame(mid_rows, m_raw, 1)
+    edges1 = send_edges(mid_rows, m_raw, 1)
     faces = mid_faces(1)
     inner0.wait_recv()
     for copy in passed0:
@@ -305,9 +310,11 @@
     pack(1)
     stats = exchange_one(1)
     faces += mid_faces(0)
-    edges0, inner0b = send_frame(mid_rows, m_raw, 0)
+    inner1b = send_inner(mid_rows, m_raw, 1)
+    edges0 = send_edges(mid_rows, m_raw, 0)
+    inner0b = send_inner(mid_rows, m_raw, 0)
+    stats = exchange_two(1, stats)
     passed1 = pass_edges(m_raw, 1, edges1)
-    stats = exchange_two(1, stats)
     params(1, stats, gain2)
     for copy in faces:
         copy.wait_recv()
@@ -372,9 +379,9 @@
             pltpu.VMEM((8, chans), F32),
             pltpu.VMEM((8, chans), F32),
             pltpu.VMEM((2, 8, 128), F32),
+            pltpu.VMEM((2, NX * NZ - 1, 8, 128), F32),
+            pltpu.VMEM((2, 8, 128), F32),
             pltpu.VMEM((2, NY * NC - 1, 8, 128), F32),
-            pltpu.VMEM((2, 8, 128), F32),
-            pltpu.VMEM((2, NX * NZ - 1, 8, 128), F32),
             pltpu.SemaphoreType.DMA((N_SENDS,)),
             pltpu.SemaphoreType.DMA((N_SENDS,)),
             pltpu.SemaphoreType.DMA((5,)),

time: 69.5 us -> 57.5 us (0.83)
  Pallas kernels: 67.4 us -> 55.3 us
    pallas_call x1, Pallas kernels: 67.4 us -> 55.3 us  [shards(): pl.pallas_call(block_kernel, out_shape=jax.ShapeDtypeStruct(latents.shape...]
where the time goes in v2:
time: 57.5 us; the launch traced here: 57.3 us
  Pallas kernels  55.3 us (96%)
  local copies, waits for them, and re-layouts  1.97 us (3%)
    pallas_call x1, Pallas kernels, shards(): pl.pallas_call(block_kernel, out_shape=jax.ShapeDtypeStruct(latents.shape...  55.3 us
    unnamed x1, local copies, waits for them, and re-layouts  1.97 us

profile of v2, /device:TPU:1, one launch (start us, length us, event | category | flops | bytes accessed | tf_op | source)
XLA Modules:
  0.0 57.3 jit_solution(1328669982976812901)
XLA Ops:
  0.0 55.3 %shard_map.64 = bf16[2,4,80,512]{3,2,1,0:T(8,128)(2,1)} custom-call(s32[4]{0:T(128)} %lengths.1, bf16[2,4,80,512]{3,2,1,0:T(8,128)(2,1)} %lat.1, bf16[3,3,3,512,512]{4,3,2,1,0:T(8,128)(2,1)} %w1_hbm.1, bf16[3,3,3,512,512]{4,3,2,1,0:T(8,128)(2,1)} %w2_hbm.1, f32[4,128]{1,0:T(4,128)} %bitcast.2, f32[4,128]{1,0:T(4,128)} %bitcast.3), custom_call_target="tpu_custom_call" | custom-call | flops 18119393280 | bytes 29622272 | tf_op jit(solution)/shard_map/pallas_call | solution.py:362
  55.3 2.0 %copy.8 = bf16[2,4,80,512]{3,2,1,0:T(8,128)(2,1)} copy(bf16[2,4,80,512]{3,2,1,0:T(8,128)(2,1)} %shard_map.64) | data formatting | bytes 1310720

commit v3 on v2

--- a/solution.py
+++ b/solution.py
@@ -32,26 +32,36 @@
 
 def block_kernel(
     lengths, lat, w1_hbm, w2_hbm, gain1, gain2, out,
-    w1, w2, x_raw, m_raw, act, acc, mid, stage, rows_scr, e_scr, p_scr, mean_scr, scale_scr,
-    src1, buf1, src2, buf2, send_sem, recv_sem, local_sem,
+    w1, w2, x_raw, m_raw, act, acc, mid, rows_scr, e_scr, p_scr, mean_scr, scale_scr,
+    buf1, buf2, send_sem, recv_sem, local_sem,
 ):
     r = lax.axis_index("req")
     t = lax.axis_index("tile")
     cells = lat.shape[1] * lat.shape[2]
     width = lat.shape[2]
-    z = t // (NY * NC)
-    yc = lax.rem(t, NY * NC)
-    right = (lax.rem(r + 1, NX), t)
+    here = NY * NC
+    yc = lax.rem(t, here)
+    plane = t - yc
+    xs = [r] + [lax.rem(r + j, NX) for j in range(1, NX)]
+    zs = [t] + [lax.rem(t + here * j, NT) for j in range(1, NZ)]
+    right = (xs[1], t)
     above = (r, lax.rem(t + NT - 1, NT))
     below = (r, lax.rem(t + 1, NT))
-    peers1 = [
-        (lax.rem(r + j // NZ, NX), lax.rem(t + (NY * NC) * (j % NZ), NT)) for j in range(1, NX * NZ)
-    ]
-    peers2 = [(r, z * (NY * NC) + lax.rem(yc + j, NY * NC)) for j in range(1, NY * NC)]
-
+    peers1 = [(xs[j // NZ], zs[j % NZ]) for j in range(1, NX * NZ)]
+    peers2 = [(r, plane + lax.rem(yc + j, here)) for j in range(1, here)]
+
+    def hops1(j):
+        return min(j // NZ, NX - j // NZ) + min(j % NZ, NZ - j % NZ)
+
+    def hops2(j):
+        return min(j // NC, NY - j // NC)
+
+    far1 = sorted(range(1, NX * NZ), key=hops1, reverse=True)
+    far2 = sorted(range(1, here), key=hops2, reverse=True)
     barrier = pltpu.get_barrier_semaphore()
-    greeted = peers1 + peers2 + [above, below]
-    for peer in greeted:
+    greeted = [(hops1(j), peers1[j - 1]) for j in far1] + [(hops2(j), peers2[j - 1]) for j in far2]
+    greeted += [(2, above), (2, below)]
+    for _, peer in sorted(greeted, key=lambda entry: entry[0], reverse=True):
         pl.semaphore_signal(barrier, inc=1, device_id=peer, device_id_type=MESH)
 
     lat_copy = pltpu.make_async_copy(lat, x_raw.at[2:4, 1:5], local_sem.at[0])
@@ -104,7 +114,7 @@
         sums = segment_sum(rows_scr[...])
         row = lax.broadcasted_iota(jnp.int32, (16, 128), 0)
         picked = jnp.where((lane_ids((16, 128)) & 15) == row, sums, 0.0)
-        src1[use] = jnp.broadcast_to(jnp.sum(picked, axis=0, keepdims=True), (8, 128))
+        buf1[use, 0:1] = jnp.sum(picked, axis=0, keepdims=True)
 
     def put_rows(frame, total, squares):
         for kind, value in enumerate((total, squares)):
@@ -114,27 +124,22 @@
                 rows_scr[k : k + 1, :] = value[:, b * 128 : (b + 1) * 128]
 
     def exchange_one(use):
-        return [send(src1.at[use], buf1.at[use, j], peer) for j, peer in enumerate(peers1)]
+        return [send(buf1.at[use, 0:1], buf1.at[use, j : j + 1], peers1[j - 1]) for j in far1]
 
     def exchange_two(use, copies):
         for copy in copies:
             copy.wait_recv()
-        row8 = lax.broadcasted_iota(jnp.int32, (8, 128), 0)
-        rows = jnp.zeros((8, 128), F32)
         for dx in range(NX):
-            total = src1[use] if dx == 0 else buf1[use, NZ * dx - 1]
-            for dz in range(1, NZ):
-                total = total + buf1[use, NZ * dx + dz - 1]
-            rows = rows + jnp.where(row8 == dx, total, 0.0)
-        src2[use] = rows
-        return [send(src2.at[use], buf2.at[use, j], peer) for j, peer in enumerate(peers2)]
+            rows = [buf1[use, j : j + 1] for j in range(NZ * dx, NZ * dx + NZ)]
+            buf2[use, 0, dx : dx + 1] = (rows[0] + rows[1]) + (rows[2] + rows[3])
+        return [send(buf2.at[use, 0], buf2.at[use, j], peers2[j - 1]) for j in far2]
 
     def params(use, copies, gain):
         for copy in copies:
             copy.wait_recv()
         lanes = lane_ids((8, 128))
-        total = src2[use]
-        for j in range(len(peers2)):
+        total = buf2[use, 0]
+        for j in range(1, here):
             total = total + buf2[use, j]
         parts = [jnp.broadcast_to(total[dx : dx + 1], (8, 128)) for dx in range(NX)]
         row8 = lax.broadcasted_iota(jnp.int32, (8, 128), 0)
@@ -261,9 +266,9 @@
         send(lat.at[0:2, 0:1], x_raw.at[2:4, 5:6], above),
         send(lat.at[0:2, 3:4], x_raw.at[2:4, 0:1], below),
     ]
+    stats = exchange_two(0, stats)
     edges0 = send_edges(lat_rows, x_raw, 0)
     inner0 = send_inner(lat_rows, x_raw, 0)
-    stats = exchange_two(0, stats)
     passed1 = pass_edges(x_raw, 1, edges1)
     params(0, stats, gain1)
     for copy in faces:
@@ -275,9 +280,9 @@
         copy.wait_recv()
     activate_rows(x_raw, 1)
     w_copies[0].wait()
-    conv(w1, 1, 0, 2)
+    conv(w1, 1, 0, 1)
     passed0 = pass_edges(x_raw, 0, edges0)
-    conv(w1, 1, 2, 3)
+    conv(w1, 1, 1, 3)
 
     def finish_mid(frame):
         def mid_row(row, carry):
@@ -311,9 +316,9 @@
     stats = exchange_one(1)
     faces += mid_faces(0)
     inner1b = send_inner(mid_rows, m_raw, 1)
+    stats = exchange_two(1, stats)
     edges0 = send_edges(mid_rows, m_raw, 0)
     inner0b = send_inner(mid_rows, m_raw, 0)
-    stats = exchange_two(1, stats)
     passed1 = pass_edges(m_raw, 1, edges1)
     params(1, stats, gain2)
     for copy in faces:
@@ -331,23 +336,18 @@
     def finish_out(frame):
         @pl.loop(0, 4)
         def _(row):
-            stage[frame, row] = (x_raw[2 + frame, row + 1].astype(F32) + conv_row(row)).astype(BF16)
-
-        copy = pltpu.make_async_copy(stage.at[frame], out.at[frame], local_sem.at[3 + frame])
-        copy.start()
-        return copy
-
-    out1 = finish_out(1)
+            out[frame, row] = (x_raw[2 + frame, row + 1].astype(F32) + conv_row(row)).astype(BF16)
+
+
+    finish_out(1)
     inner0b.wait_recv()
     for copy in passed0:
         copy.wait_recv()
     activate_rows(m_raw, 0)
     conv(w2, 0, 0, 3)
-    out0 = finish_out(0)
+    finish_out(0)
     for copy in sent:
         copy.wait_send()
-    out1.wait()
-    out0.wait()
 
 
 N_SENDS = 2 * (NY * NC - 1) + 2 * (NX * NZ - 1) + 12 + 6 + 8
@@ -361,9 +361,9 @@
     flops = 2 * 2 * frames * rows * width * 27 * chans * chans
     return pl.pallas_call(
         block_kernel,
-        out_shape=jax.ShapeDtypeStruct(latents.shape, latents.dtype),
+        out_shape=pltpu.VMEM(latents.shape, latents.dtype),
         in_specs=[smem, hbm, hbm, hbm, vmem, vmem],
-        out_specs=hbm,
+        out_specs=pl.BlockSpec(memory_space=pltpu.VMEM),
         scratch_shapes=[
             pltpu.VMEM(conv_first.shape, BF16),
             pltpu.VMEM(conv_second.shape, BF16),
@@ -372,19 +372,16 @@
             pltpu.VMEM((3, 2, rows + 2, width, chans), BF16),
             pltpu.VMEM((3, rows * width, chans), F32),
             pltpu.VMEM((2, rows, width, chans), F32),
-            pltpu.VMEM((2, rows, width, chans), BF16),
             pltpu.VMEM((16, 128), F32),
             pltpu.VMEM((32, 128), F32),
             pltpu.VMEM((32, 128), F32),
             pltpu.VMEM((8, chans), F32),
             pltpu.VMEM((8, chans), F32),
-            pltpu.VMEM((2, 8, 128), F32),
-            pltpu.VMEM((2, NX * NZ - 1, 8, 128), F32),
-            pltpu.VMEM((2, 8, 128), F32),
-            pltpu.VMEM((2, NY * NC - 1, 8, 128), F32),
+            pltpu.VMEM((2, NX * NZ, 128), F32),
+            pltpu.VMEM((2, NY * NC, NX, 128), F32),
             pltpu.SemaphoreType.DMA((N_SENDS,)),
             pltpu.SemaphoreType.DMA((N_SENDS,)),
-            pltpu.SemaphoreType.DMA((5,)),
+            pltpu.SemaphoreType.DMA((3,)),
         ],
         compiler_params=pltpu.CompilerParams(
             collective_id=0, has_side_effects=True, vmem_limit_bytes=60 * 2**20

time: 57.5 us -> 55.1 us (0.958)
  Pallas kernels: 55.3 us -> 53.8 us
  local copies, waits for them, and re-layouts: 1.97 us -> 0.84 us
    pallas_call x1, Pallas kernels: 55.3 us -> 53.8 us  [shards(): pl.pallas_call(block_kernel, out_shape=pltpu.VMEM(latents.shape, latents....]
    unnamed x1, local copies, waits for them, and re-layouts: 1.97 us -> 0.84 us
where the time goes in v3:
time: 55.1 us; the launch traced here: 54.6 us
  Pallas kernels  53.8 us (98%)
  local copies, waits for them, and re-layouts  0.84 us (2%)
    pallas_call x1, Pallas kernels, shards(): pl.pallas_call(block_kernel, out_shape=pltpu.VMEM(latents.shape, latents....  53.8 us

profile of v3, /device:TPU:1, one launch (start us, length us, event | category | flops | bytes accessed | tf_op | source)
XLA Modules:
  0.0 54.6 jit_solution(300041581863454591)
XLA Ops:
  0.0 53.8 %shard_map.64 = bf16[2,4,80,512]{3,2,1,0:T(8,128)(2,1)S(1)} custom-call(s32[4]{0:T(128)} %lengths.1, bf16[2,4,80,512]{3,2,1,0:T(8,128)(2,1)} %lat.1, bf16[3,3,3,512,512]{4,3,2,1,0:T(8,128)(2,1)} %w1_hbm.1, bf16[3,3,3,512,512]{4,3,2,1,0:T(8,128)(2,1)} %w2_hbm.1, f32[4,128]{1,0:T(4,128)} %bitcast.2, f32[4,128]{1,0:T(4,128)} %bitcast.3), custom_call_target="tpu_custom_call" | custom-call | flops 18119393280 | bytes 29622272 | tf_op jit(solution)/shard_map/pallas_call | solution.py:362
  53.8 0.8 %copy.8 = bf16[2,4,80,512]{3,2,1,0:T(8,128)(2,1)} copy(bf16[2,4,80,512]{3,2,1,0:T(8,128)(2,1)S(1)} %shard_map.64) | data formatting | bytes 1310720

commit v4 on v3

--- a/solution.py
+++ b/solution.py
@@ -33,7 +33,7 @@
 def block_kernel(
     lengths, lat, w1_hbm, w2_hbm, gain1, gain2, out,
     w1, w2, x_raw, m_raw, act, acc, mid, rows_scr, e_scr, p_scr, mean_scr, scale_scr,
-    buf1, buf2, send_sem, recv_sem, local_sem,
+    buf0, buf1, send_sem, recv_sem, chip_sem, local_sem,
 ):
     r = lax.axis_index("req")
     t = lax.axis_index("tile")
@@ -41,28 +41,33 @@
     width = lat.shape[2]
     here = NY * NC
     yc = lax.rem(t, here)
+    core = lax.rem(t, NC)
     plane = t - yc
     xs = [r] + [lax.rem(r + j, NX) for j in range(1, NX)]
-    zs = [t] + [lax.rem(t + here * j, NT) for j in range(1, NZ)]
+    planes = [plane] + [lax.rem(plane + here * j, NT) for j in range(1, NZ)]
+    ys = [yc] + [lax.rem(yc + NC * j, here) for j in range(1, NY)]
     right = (xs[1], t)
+    sibling = (r, t + 1 - 2 * core)
     above = (r, lax.rem(t + NT - 1, NT))
     below = (r, lax.rem(t + 1, NT))
-    peers1 = [(xs[j // NZ], zs[j % NZ]) for j in range(1, NX * NZ)]
-    peers2 = [(r, plane + lax.rem(yc + j, here)) for j in range(1, here)]
-
-    def hops1(j):
-        return min(j // NZ, NX - j // NZ) + min(j % NZ, NZ - j % NZ)
-
-    def hops2(j):
-        return min(j // NC, NY - j // NC)
-
-    far1 = sorted(range(1, NX * NZ), key=hops1, reverse=True)
-    far2 = sorted(range(1, here), key=hops2, reverse=True)
+    chips = NX * NY * NZ
+
+    def steps(j):
+        return j // (NY * NZ), (j // NZ) % NY, j % NZ
+
+    def hops(j):
+        dx, dy, dz = steps(j)
+        return min(dx, NX - dx) + min(dy, NY - dy) + min(dz, NZ - dz)
+
+    def peer(j):
+        dx, dy, dz = steps(j)
+        return (xs[dx], planes[dz] + ys[dy])
+
+    far = sorted(range(1, chips), key=hops, reverse=True)
     barrier = pltpu.get_barrier_semaphore()
-    greeted = [(hops1(j), peers1[j - 1]) for j in far1] + [(hops2(j), peers2[j - 1]) for j in far2]
-    greeted += [(2, above), (2, below)]
-    for _, peer in sorted(greeted, key=lambda entry: entry[0], reverse=True):
-        pl.semaphore_signal(barrier, inc=1, device_id=peer, device_id_type=MESH)
+    greeted = [peer(j) for j in far] + [above, below, sibling]
+    for other in greeted:
+        pl.semaphore_signal(barrier, inc=1, device_id=other, device_id_type=MESH)
 
     lat_copy = pltpu.make_async_copy(lat, x_raw.at[2:4, 1:5], local_sem.at[0])
     lat_copy.start()
@@ -114,7 +119,7 @@
         sums = segment_sum(rows_scr[...])
         row = lax.broadcasted_iota(jnp.int32, (16, 128), 0)
         picked = jnp.where((lane_ids((16, 128)) & 15) == row, sums, 0.0)
-        buf1[use, 0:1] = jnp.sum(picked, axis=0, keepdims=True)
+        buf0[use, 0:1] = jnp.sum(picked, axis=0, keepdims=True)
 
     def put_rows(frame, total, squares):
         for kind, value in enumerate((total, squares)):
@@ -124,24 +129,31 @@
                 rows_scr[k : k + 1, :] = value[:, b * 128 : (b + 1) * 128]
 
     def exchange_one(use):
-        return [send(buf1.at[use, 0:1], buf1.at[use, j : j + 1], peers1[j - 1]) for j in far1]
-
-    def exchange_two(use, copies):
-        for copy in copies:
-            copy.wait_recv()
+        return send(buf0.at[use, 0:1], buf0.at[use, 1:2], sibling)
+
+    def rows_of_others(use):
+        return buf1.at[use, 1:chips]
+
+    def exchange_two(use, copy):
+        copy.wait_recv()
+        buf1[use, 0:1] = buf0[use, 0:1] + buf0[use, 1:2]
+        for j in far:
+            pltpu.make_async_remote_copy(
+                src_ref=buf1.at[use, 0:1], dst_ref=buf1.at[use, j : j + 1], send_sem=chip_sem.at[use],
+                recv_sem=chip_sem.at[2 + use], device_id=peer(j), device_id_type=MESH,
+            ).start()
+
+    def chips_done(use, sem):
+        pltpu.make_async_copy(rows_of_others(use), rows_of_others(use), chip_sem.at[sem]).wait()
+
+    def params(use, gain):
+        chips_done(use, 2 + use)
+        lanes = lane_ids((8, 128))
+        per_x = NY * NZ
+        parts = []
         for dx in range(NX):
-            rows = [buf1[use, j : j + 1] for j in range(NZ * dx, NZ * dx + NZ)]
-            buf2[use, 0, dx : dx + 1] = (rows[0] + rows[1]) + (rows[2] + rows[3])
-        return [send(buf2.at[use, 0], buf2.at[use, j], peers2[j - 1]) for j in far2]
-
-    def params(use, copies, gain):
-        for copy in copies:
-            copy.wait_recv()
-        lanes = lane_ids((8, 128))
-        total = buf2[use, 0]
-        for j in range(1, here):
-            total = total + buf2[use, j]
-        parts = [jnp.broadcast_to(total[dx : dx + 1], (8, 128)) for dx in range(NX)]
+            total = jnp.sum(buf1[use, dx * per_x : (dx + 1) * per_x], axis=0, keepdims=True)
+            parts.append(jnp.broadcast_to(total, (8, 128)))
         row8 = lax.broadcasted_iota(jnp.int32, (8, 128), 0)
         early = (lanes & 8) == 0
         for q in range(4):
@@ -258,19 +270,19 @@
     stats = exchange_one(0)
 
     def lat_rows(frame, row, n):
-        return lat.at[frame, row : row + n]
+        return x_raw.at[2 + frame, row + 1 : row + 1 + n]
 
     edges1 = send_edges(lat_rows, x_raw, 1)
-    inner1 = send_inner(lat_rows, x_raw, 1)
+    exchange_two(0, stats)
     faces = [
         send(lat.at[0:2, 0:1], x_raw.at[2:4, 5:6], above),
         send(lat.at[0:2, 3:4], x_raw.at[2:4, 0:1], below),
     ]
-    stats = exchange_two(0, stats)
+    inner1 = send_inner(lat_rows, x_raw, 1)
     edges0 = send_edges(lat_rows, x_raw, 0)
     inner0 = send_inner(lat_rows, x_raw, 0)
     passed1 = pass_edges(x_raw, 1, edges1)
-    params(0, stats, gain1)
+    params(0, gain1)
     for copy in faces:
         copy.wait_recv()
     activate_rows(x_raw, 3)
@@ -305,6 +317,7 @@
 
     finish_mid(1)
     edges1 = send_edges(mid_rows, m_raw, 1)
+    inner1b = send_inner(mid_rows, m_raw, 1)
     faces = mid_faces(1)
     inner0.wait_recv()
     for copy in passed0:
@@ -314,13 +327,12 @@
     finish_mid(0)
     pack(1)
     stats = exchange_one(1)
+    exchange_two(1, stats)
     faces += mid_faces(0)
-    inner1b = send_inner(mid_rows, m_raw, 1)
-    stats = exchange_two(1, stats)
     edges0 = send_edges(mid_rows, m_raw, 0)
     inner0b = send_inner(mid_rows, m_raw, 0)
     passed1 = pass_edges(m_raw, 1, edges1)
-    params(1, stats, gain2)
+    params(1, gain2)
     for copy in faces:
         copy.wait_recv()
     activate_wide(3)
@@ -348,9 +360,11 @@
     finish_out(0)
     for copy in sent:
         copy.wait_send()
-
-
-N_SENDS = 2 * (NY * NC - 1) + 2 * (NX * NZ - 1) + 12 + 6 + 8
+    for use in range(2):
+        chips_done(use, use)
+
+
+N_SENDS = 2 + 12 + 6 + 8
 
 
 def shards(latents, lengths, conv_first, conv_second, gain_first, gain_second):
@@ -377,10 +391,11 @@
             pltpu.VMEM((32, 128), F32),
             pltpu.VMEM((8, chans), F32),
             pltpu.VMEM((8, chans), F32),
-            pltpu.VMEM((2, NX * NZ, 128), F32),
-            pltpu.VMEM((2, NY * NC, NX, 128), F32),
+            pltpu.VMEM((2, 8, 128), F32),
+            pltpu.VMEM((2, NX * NY * NZ, 128), F32),
             pltpu.SemaphoreType.DMA((N_SENDS,)),
             pltpu.SemaphoreType.DMA((N_SENDS,)),
+            pltpu.SemaphoreType.DMA((4,)),
             pltpu.SemaphoreType.DMA((3,)),
         ],
         compiler_params=pltpu.CompilerParams(

time: 55.1 us -> 54.1 us (0.982)
  Pallas kernels: 53.8 us -> 52.8 us
    pallas_call x1, Pallas kernels: 53.8 us -> 52.8 us  [shards(): pl.pallas_call(block_kernel, out_shape=pltpu.VMEM(latents.shape, latents....]
where the time goes in v4:
time: 54.1 us; the launch traced here: 53.7 us
  Pallas kernels  52.8 us (98%)
  local copies, waits for them, and re-layouts  0.84 us (2%)
    pallas_call x1, Pallas kernels, shards(): pl.pallas_call(block_kernel, out_shape=pltpu.VMEM(latents.shape, latents....  52.8 us

profile of v4, /device:TPU:1, one launch (start us, length us, event | category | flops | bytes accessed | tf_op | source)
XLA Modules:
  0.0 53.7 jit_solution(11206449451373424938)
XLA Ops:
  0.0 52.8 %shard_map.64 = bf16[2,4,80,512]{3,2,1,0:T(8,128)(2,1)S(1)} custom-call(s32[4]{0:T(128)} %lengths.1, bf16[2,4,80,512]{3,2,1,0:T(8,128)(2,1)} %lat.1, bf16[3,3,3,512,512]{4,3,2,1,0:T(8,128)(2,1)} %w1_hbm.1, bf16[3,3,3,512,512]{4,3,2,1,0:T(8,128)(2,1)} %w2_hbm.1, f32[4,128]{1,0:T(4,128)} %bitcast.2, f32[4,128]{1,0:T(4,128)} %bitcast.3), custom_call_target="tpu_custom_call" | custom-call | flops 18119393280 | bytes 29622272 | tf_op jit(solution)/shard_map/pallas_call | solution.py:376
  52.8 0.8 %copy.8 = bf16[2,4,80,512]{3,2,1,0:T(8,128)(2,1)} copy(bf16[2,4,80,512]{3,2,1,0:T(8,128)(2,1)S(1)} %shard_map.64) | data formatting | bytes 1310720

commit v5 on v4

--- a/solution.py
+++ b/solution.py
@@ -260,12 +260,10 @@
         return send(src_rows(frame, 1, 2), dst.at[frame, 2:4], right)
 
     def pass_edges(dst, q, edges):
-        for edge in edges:
-            edge.wait_recv()
-        return [
-            send(dst.at[q, 1:2], dst.at[q, 5:6], above),
-            send(dst.at[q, 4:5], dst.at[q, 0:1], below),
-        ]
+        edges[0].wait_recv()
+        up = send(dst.at[q, 1:2], dst.at[q, 5:6], above)
+        edges[1].wait_recv()
+        return [up, send(dst.at[q, 4:5], dst.at[q, 0:1], below)]
 
     stats = exchange_one(0)
 

time: 54.1 us -> 53.4 us (0.987)
  no operation moved by 1% of the time
where the time goes in v5:
time: 53.4 us; the launch traced here: 53.2 us
  Pallas kernels  52.4 us (98%)
  local copies, waits for them, and re-layouts  0.84 us (2%)
    pallas_call x1, Pallas kernels, shards(): pl.pallas_call(block_kernel, out_shape=pltpu.VMEM(latents.shape, latents....  52.4 us

profile of v5, /device:TPU:1, one launch (start us, length us, event | category | flops | bytes accessed | tf_op | source)
XLA Modules:
  0.0 53.2 jit_solution(16725739102502325455)
XLA Ops:
  0.0 52.4 %shard_map.64 = bf16[2,4,80,512]{3,2,1,0:T(8,128)(2,1)S(1)} custom-call(s32[4]{0:T(128)} %lengths.1, bf16[2,4,80,512]{3,2,1,0:T(8,128)(2,1)} %lat.1, bf16[3,3,3,512,512]{4,3,2,1,0:T(8,128)(2,1)} %w1_hbm.1, bf16[3,3,3,512,512]{4,3,2,1,0:T(8,128)(2,1)} %w2_hbm.1, f32[4,128]{1,0:T(4,128)} %bitcast.2, f32[4,128]{1,0:T(4,128)} %bitcast.3), custom_call_target="tpu_custom_call" | custom-call | flops 18119393280 | bytes 29622272 | tf_op jit(solution)/shard_map/pallas_call | solution.py:374
  52.4 0.8 %copy.8 = bf16[2,4,80,512]{3,2,1,0:T(8,128)(2,1)} copy(bf16[2,4,80,512]{3,2,1,0:T(8,128)(2,1)S(1)} %shard_map.64) | data formatting | bytes 1310720

commit v6 on v5

--- a/solution.py
+++ b/solution.py
@@ -276,8 +276,8 @@
         send(lat.at[0:2, 0:1], x_raw.at[2:4, 5:6], above),
         send(lat.at[0:2, 3:4], x_raw.at[2:4, 0:1], below),
     ]
+    edges0 = send_edges(lat_rows, x_raw, 0)
     inner1 = send_inner(lat_rows, x_raw, 1)
-    edges0 = send_edges(lat_rows, x_raw, 0)
     inner0 = send_inner(lat_rows, x_raw, 0)
     passed1 = pass_edges(x_raw, 1, edges1)
     params(0, gain1)

time: 53.4 us -> 56.2 us (1.052)
  Pallas kernels: 52.4 us -> 54.7 us
    pallas_call x1, Pallas kernels: 52.4 us -> 54.7 us  [shards(): pl.pallas_call(block_kernel, out_shape=pltpu.VMEM(latents.shape, latents....]
where the time goes in v6:
time: 56.2 us; the launch traced here: 55.5 us
  Pallas kernels  54.7 us (97%)
  local copies, waits for them, and re-layouts  0.84 us (1%)
    pallas_call x1, Pallas kernels, shards(): pl.pallas_call(block_kernel, out_shape=pltpu.VMEM(latents.shape, latents....  54.7 us

profile of v6, /device:TPU:1, one launch (start us, length us, event | category | flops | bytes accessed | tf_op | source)
XLA Modules:
  0.0 55.5 jit_solution(4178791765149059554)
XLA Ops:
  0.0 54.7 %shard_map.64 = bf16[2,4,80,512]{3,2,1,0:T(8,128)(2,1)S(1)} custom-call(s32[4]{0:T(128)} %lengths.1, bf16[2,4,80,512]{3,2,1,0:T(8,128)(2,1)} %lat.1, bf16[3,3,3,512,512]{4,3,2,1,0:T(8,128)(2,1)} %w1_hbm.1, bf16[3,3,3,512,512]{4,3,2,1,0:T(8,128)(2,1)} %w2_hbm.1, f32[4,128]{1,0:T(4,128)} %bitcast.2, f32[4,128]{1,0:T(4,128)} %bitcast.3), custom_call_target="tpu_custom_call" | custom-call | flops 18119393280 | bytes 29622272 | tf_op jit(solution)/shard_map/pallas_call | solution.py:374
  54.7 0.8 %copy.8 = bf16[2,4,80,512]{3,2,1,0:T(8,128)(2,1)} copy(bf16[2,4,80,512]{3,2,1,0:T(8,128)(2,1)S(1)} %shard_map.64) | data formatting | bytes 1310720
